TPU v7x, 32 devices: a whole 2x2x4 slice. The times are simulated.
32 devices in a mesh: mem: 4 (over z), lat: 8 (over y, x, core).
Axes of the slice: x: 2, y: 2, z: 4, core: 2. Of those that a mesh axis runs over, the one named last changes fastest.
Arguments:
- v_fine: float32 [128, 1024], P('lat'), may hold values from -6 to 6
- v_coarse: float32 [256, 256], P('lat'), may hold values from -6 to 6
- pert_fine: bfloat16 [64, 128, 1024], P('mem', 'lat'), may hold values from -6 to 6
- pert_coarse: bfloat16 [64, 256, 256], P('mem', 'lat'), may hold values from -6 to 6
- gauss_lat: bfloat16 [256, 256], replicated, may hold values from 0 to 0.5629165, as said below
- gauss_lon: bfloat16 [256, 256], replicated, may hold values from 0 to 1.0277402, as said below
Outputs:
- fine_increment: float32 [128, 1024], P('lat')
- coarse_increment: float32 [256, 256], P('lat')
Inputs may be any that keep to these rules, and one draw needn't show every extreme that they name: `gauss_lat`: nonnegative entries. `gauss_lon`: nonnegative entries.
All inputs are finite; a program needn't handle non-finite values.
Results may differ from a plain program's by a relative error of at most 0.005.
Values may be sent and summed in bfloat16 or wider, within the bound.
A program may use at most 64 MiB of HBM per device.

v0:
```python
import math

import jax
import jax.numpy as jnp
from jax import lax
from jax.sharding import PartitionSpec as P


def extended(shard, sides, width):
    for axis, dim in sides:
        count, length = (lax.axis_size(axis), shard.shape[dim])
        up = [(i, (i + 1) % count) for i in range(count - 1)]
        down = [(j, i) for i, j in up]
        last = lax.slice_in_dim(shard, length - width, length, axis=dim)
        leading = lax.slice_in_dim(shard, 0, width, axis=dim)
        before = lax.ppermute(last, axis, up)
        after = lax.ppermute(leading, axis, down)
        shard = jnp.concatenate([before, shard, after], axis=dim)
    return shard


def fine_taps():
    return [math.exp(-(offset - 5) * (offset - 5) / 32.0) for offset in range(11)]


def local(v_fine, v_coarse, pert_fine, pert_coarse, gauss_lat, gauss_lon):
    taps = fine_taps()
    count = pert_fine.shape[0]
    members = count * lax.axis_size("mem")
    rows = pert_fine.shape[1]
    weighted = (pert_fine.astype(jnp.float32) * v_fine[None]).astype(jnp.bfloat16)
    padded = extended(weighted, (("lat", 1),), 5)
    along = taps[0] * padded[:, 0:rows].astype(jnp.float32)
    for offset in range(1, 11):
        along = along + taps[offset] * padded[:, offset : offset + rows].astype(jnp.float32)
    across = taps[0] * jnp.roll(along, -5, axis=2)
    for offset in range(1, 11):
        across = across + taps[offset] * jnp.roll(along, offset - 5, axis=2)
    fine_part = jnp.sum(pert_fine.astype(jnp.float32) * across, axis=0)
    crows = pert_coarse.shape[1]
    cwidth = pert_coarse.shape[2]
    cweighted = (pert_coarse.astype(jnp.float32) * v_coarse[None]).astype(jnp.bfloat16)
    flat_rows = cweighted.reshape(count * crows, cwidth)
    ctrans = jnp.einsum("rc,dc->rd", flat_rows, gauss_lon, preferred_element_type=jnp.float32)
    ctrans = ctrans.astype(jnp.bfloat16).reshape(count, crows, cwidth)
    band = lax.dynamic_slice_in_dim(gauss_lat, lax.axis_index("lat") * crows, crows, 0)
    smooth = jnp.einsum(
        "rj,mjc->mrc",
        band,
        lax.all_gather(ctrans, "lat", axis=1, tiled=True),
        preferred_element_type=jnp.float32,
    ).astype(jnp.bfloat16)
    coarse_part = jnp.sum(pert_coarse.astype(jnp.float32) * smooth.astype(jnp.float32), axis=0)
    fine_total, coarse_total = lax.psum((fine_part, coarse_part), "mem")
    factor = 1.0 / (members - 1)
    return (fine_total * factor, coarse_total * factor)


def solution(mesh):
    placed = (
        P("lat", None),
        P("lat", None),
        P("mem", "lat", None),
        P("mem", "lat", None),
        P(),
        P(),
    )
    return jax.shard_map(
        local,
        mesh=mesh,
        in_specs=placed,
        out_specs=(P("lat", None), P("lat", None)),
        check_vma=False,
    )
```

profile of v0, /device:TPU:0, one launch (start us, length us, event | category | flops | bytes accessed | tf_op | source)
XLA Modules:
  0.0 94.8 jit_solution(11587460546678524564)
XLA Ops:
  8.0 0.0 copy-start
  8.0 0.0 all-reduce.2.cloned.1.call-start
  8.1 1.2 %fusion.4 = bf16[16,16,1024]{2,1,0:T(8,128)(2,1)S(1)} fusion(bf16[16,16,1024]{2,1,0:T(8,128)(2,1)} %param.8, f32[16,1024]{1,0:T(8,128)} %param.6), kind=kLoop, calls=%fused_computation.16 | loop fusion | flops 786432 | bytes 1114112 | tf_op jit(solution)/shard_map/convert_element_type | solution.py:31
  9.3 0.1 fusion.38
  9.4 2.4 %collective-permute-start = (bf16[16,5,1024]{2,1,0:T(8,128)(2,1)S(1)}, bf16[16,5,1024]{2,1,0:T(8,128)(2,1)S(1)}, u32[]{:S(2)}, u32[]{:S(2)}) collective-permute-start(bf16[16,5,1024]{2,1,0:T(8,128)(2,1)S(1)} %get-tuple-element.22), channel_id=1, source_target_pairs={{0,1},{1,2},{2,3},{3,4},{4,5},{5,6},{6,7},{8,9},{9,10},{10,11},{11... | collective-permute-start | bytes 491528 | tf_op jit(solution)/shard_map/ppermute | solution.py:16
  11.8 1.3 %collective-permute-start.1 = (bf16[16,5,1024]{2,1,0:T(8,128)(2,1)S(1)}, bf16[16,5,1024]{2,1,0:T(8,128)(2,1)S(1)}, u32[]{:S(2)}, u32[]{:S(2)}) collective-permute-start(bf16[16,5,1024]{2,1,0:T(8,128)(2,1)S(1)} %get-tuple-element.23), channel_id=1, source_target_pairs={{1,0},{2,1},{3,2},{4,3},{5,4},{6,5},{7,6},{9,8},{10,9},{11,10},{12... | collective-permute-start | bytes 491528 | tf_op jit(solution)/shard_map/ppermute | solution.py:17
  13.1 0.1 fusion.16
  13.2 0.0 collective-permute-done
  13.2 4.1 %collective-permute-done.1 = bf16[16,5,1024]{2,1,0:T(8,128)(2,1)S(1)} collective-permute-done((bf16[16,5,1024]{2,1,0:T(8,128)(2,1)S(1)}, bf16[16,5,1024]{2,1,0:T(8,128)(2,1)S(1)}, u32[]{:S(2)}, u32[]{:S(2)}) %collective-permute-start.1) | collective-permute-done | bytes 163872 | tf_op jit(solution)/shard_map/ppermute | solution.py:17
  17.3 2.1 %multiply_add_fusion = f32[16,16,1024]{2,1,0:T(8,128)S(1)} fusion(bf16[16,16,1024]{2,1,0:T(8,128)(2,1)S(1)} %fusion.4, bf16[16,5,1024]{2,1,0:T(8,128)(2,1)S(1)} %collective-permute-done.1, bf16[16,5,1024]{2,1,0:T(8,128)(2,1)S(1)} %collective-permute-done), kind=kLoop, calls=%fused_computation.38 | loop fusion | flops 15990784 | bytes 1900544 | tf_op jit(solution)/shard_map/add | solution.py:35
  19.4 0.4 fusion.33
  19.8 0.4 fusion.35
  20.2 0.4 fusion.37
  20.6 0.4 fusion.29
  21.0 0.4 fusion.31
  21.4 0.0 copy-start.1
  21.4 0.1 fusion.32
  21.5 0.1 fusion.34
  21.6 0.1 fusion.36
  21.7 0.1 fusion.28
  21.8 0.1 fusion.30
  21.9 0.5 copy-done.1
  22.4 3.2 %fusion.5 = f32[16,1024]{1,0:T(8,128)} fusion(bf16[16,16,1024]{2,1,0:T(8,128)(2,1)S(1)} %copy-done.1, f32[16,16,1024]{2,1,0:T(8,128)S(1)} %multiply_add_fusion, f32[16,16,5]{2,1,0:T(8,128)S(1)} %get-tuple-element.3, f32[16,16,1019]{2,1,0:T(8,128)S(1)} %get-tuple-element.5, f32[16,16,4]{2,1,0:T(8,128)S(1)} %get-tuple-element.7, ...), kind=kLoop, calls=%fused_computation.17 | loop fusion | flops 8634368 | bytes 12124160 | tf_op jit(solution)/shard_map/reduce_sum | solution.py:39
  25.6 0.0 all-reduce.2.cloned.1.call-update
  25.6 0.0 all-gather.2.cloned.1.call-start
  25.7 1.0 %convolution_convert_fusion.1 = bf16[512,256]{1,0:T(8,128)(2,1)} fusion(bf16[512,256]{1,0:T(8,128)(2,1)S(1)} %bitcast.14, bf16[256,256]{1,0:T(8,128)(2,1)S(1)} %copy-done), kind=kOutput, calls=%fused_computation.14 | convolution fusion | flops 67239936 | bytes 655360 | tf_op jit(solution)/shard_map/rc,dc->rd/dot_general | solution.py:44
  26.6 0.0 all-gather.2.cloned.1.call-update
  26.7 38.7 %all-reduce.2.cloned.1.call-done = f32[16,1024]{1,0:T(8,128)} async-done(((f32[16,1024]{1,0:T(8,128)}), f32[16,1024]{1,0:T(8,128)}) %all-reduce.2.cloned.1.call-update) | async-done | bytes 65552 | tf_op jit(solution)/shard_map/psum | solution.py:54
  65.4 1.5 %broadcast_multiply_fusion = f32[16,1024]{1,0:T(8,128)} fusion(f32[16,1024]{1,0:T(8,128)} %all-reduce.2.cloned.1.call-done), kind=kLoop, calls=%fused_computation.59 | loop fusion | flops 16384 | bytes 131072 | tf_op jit(solution)/shard_map/mul | solution.py:56
  66.9 2.1 %fusion.3 = f32[32,256]{1,0:T(8,128)S(1)} fusion(bf16[16,256,256]{2,1,0:T(8,128)(2,1)} %all-gather.2.cloned.1.call-done, bf16[16,32,256]{2,1,0:T(8,128)(2,1)S(1)} %copy-done.2, bf16[256,256]{1,0:T(8,128)(2,1)} %param.10, s32[]{:T(128)S(6)} %select_n.3), kind=kOutput, calls=%fused_computation.15 | convolution fusion | flops 67756032 | bytes 2408452 | tf_op jit(solution)/shard_map/rj,mjc->mrc/dot_general | solution.py:47
  69.0 17.8 %psum.15 = f32[32,256]{1,0:T(8,128)S(1)} all-reduce(f32[32,256]{1,0:T(8,128)S(1)} %fusion.3), channel_id=1, replica_groups=mesh['mem'=4,'lat'=8] {'mem'}, use_global_device_ids=true, to_apply=%region_3.4 | all-reduce | flops 8192 | bytes 65536 | tf_op jit(solution)/shard_map/psum | solution.py:54
  86.7 0.6 broadcast_multiply_fusion.1
  (6 shorter events, 0.0 us)
Async XLA Ops:
  8.0 17.7 %copy-start = (bf16[256,256]{1,0:T(8,128)(2,1)S(1)}, bf16[256,256]{1,0:T(8,128)(2,1)}, u32[]{:S(2)}) copy-start(bf16[256,256]{1,0:T(8,128)(2,1)} %param.11) | copy-start | bytes 393220
  8.0 5.1 %copy-start.3 = (f32[32,256]{1,0:T(8,128)S(1)}, f32[32,256]{1,0:T(8,128)}, u32[]{:S(2)}) copy-start(f32[32,256]{1,0:T(8,128)} %param.7) | copy-start | bytes 98308
  8.0 5.1 %copy-start.2 = (bf16[16,32,256]{2,1,0:T(8,128)(2,1)S(1)}, bf16[16,32,256]{2,1,0:T(8,128)(2,1)}, u32[]{:S(2)}) copy-start(bf16[16,32,256]{2,1,0:T(8,128)(2,1)} %param.9) | copy-start | bytes 786436
  8.0 57.4 %all-reduce.2.cloned.1.call-start = ((), (), s32[]{:S(2)}) async-start(), calls=%async_computation | async-start | bytes 131072 | tf_op jit(solution)/shard_map/psum | solution.py:54
  9.4 3.8 %collective-permute-start = (bf16[16,5,1024]{2,1,0:T(8,128)(2,1)S(1)}, bf16[16,5,1024]{2,1,0:T(8,128)(2,1)S(1)}, u32[]{:S(2)}, u32[]{:S(2)}) collective-permute-start(bf16[16,5,1024]{2,1,0:T(8,128)(2,1)S(1)} %get-tuple-element.22), channel_id=1, source_target_pairs={{0,1},{1,2},{2,3},{3,4},{4,5},{5,6},{6,7},{8,9},{9,10},{10,11},{11... | collective-permute-start | bytes 491528 | tf_op jit(solution)/shard_map/ppermute | solution.py:16
  11.8 5.5 %collective-permute-start.1 = (bf16[16,5,1024]{2,1,0:T(8,128)(2,1)S(1)}, bf16[16,5,1024]{2,1,0:T(8,128)(2,1)S(1)}, u32[]{:S(2)}, u32[]{:S(2)}) collective-permute-start(bf16[16,5,1024]{2,1,0:T(8,128)(2,1)S(1)} %get-tuple-element.23), channel_id=1, source_target_pairs={{1,0},{2,1},{3,2},{4,3},{5,4},{6,5},{7,6},{9,8},{10,9},{11,10},{12... | collective-permute-start | bytes 491528 | tf_op jit(solution)/shard_map/ppermute | solution.py:17
  21.4 1.0 %copy-start.1 = (bf16[16,16,1024]{2,1,0:T(8,128)(2,1)S(1)}, bf16[16,16,1024]{2,1,0:T(8,128)(2,1)}, u32[]{:S(2)}) copy-start(bf16[16,16,1024]{2,1,0:T(8,128)(2,1)} %param.8) | copy-start | bytes 1572868
  25.6 41.2 %all-gather.2.cloned.1.call-start = ((), (), s32[]{:S(2)}) async-start(), calls=%async_computation.1 | async-start | bytes 2359296 | tf_op jit(solution)/shard_map/all_gather | solution.py:50
Sparse Core Ops, SparseCore 0:
  25.7 39.5 all-reduce.1
Sparse Core Ops, SparseCore 1:
  28.2 33.3 all-gather.1
where the time goes:
time: 95.1 us; the launch traced here: 94.8 us
  waiting for transfers between devices  42.9 us (45%)
  blocking collectives  17.8 us (19%)
  between operations  15.7 us (17%)
  other arithmetic  8.65 us (9%)
  starting transfers between devices  3.75 us (4%)
  local copies, waits for them, and re-layouts  3.03 us (3%)
  matrix products  3.03 us (3%)
    psum x1, waiting for transfers between devices, local(): fine_total, coarse_total = lax.psum((fine_part, coarse_part), 'mem')  38.7 us
    psum x1, blocking collectives, local(): fine_total, coarse_total = lax.psum((fine_part, coarse_part), 'mem')  17.8 us
    ppermute x1, waiting for transfers between devices, extended(): after = lax.ppermute(leading, axis, down)  4.13 us
    reduce_sum x1, other arithmetic, local(): fine_part = jnp.sum(pert_fine.astype(jnp.float32) * across, axis=0)  3.19 us
    slice x10, local copies, waits for them, and re-layouts, local(): across = across + taps[offset] * jnp.roll(along, offset - 5, axis=2)  2.41 us
    ppermute x1, starting transfers between devices, extended(): before = lax.ppermute(last, axis, up)  2.37 us
    add x1, other arithmetic, local(): along + taps[offset] * padded[:, offset:offset + rows].astype(jnp.float32)  2.09 us
    mul x2, other arithmetic, local(): return (fine_total * factor, coarse_total * factor)  2.09 us
  transfers between devices with their start and end apart: 4, of which 2 were waited for; matrix products, arithmetic and copies ran while one was open for 3% of the time, Pallas kernels for 0%

commit v1 on v0

--- a/solution.py
+++ b/solution.py
@@ -1,9 +1,18 @@
+import functools
 import math
 
 import jax
 import jax.numpy as jnp
+import numpy as np
 from jax import lax
+from jax.experimental import pallas as pl
+from jax.experimental.pallas import tpu as pltpu
 from jax.sharding import PartitionSpec as P
+
+REACH = 5
+MESH = pl.DeviceIdType.MESH
+F32 = jnp.float32
+BF16 = jnp.bfloat16
 
 
 def extended(shard, sides, width):
@@ -23,7 +32,7 @@
     return [math.exp(-(offset - 5) * (offset - 5) / 32.0) for offset in range(11)]
 
 
-def local(v_fine, v_coarse, pert_fine, pert_coarse, gauss_lat, gauss_lon):
+def general(v_fine, v_coarse, pert_fine, pert_coarse, gauss_lat, gauss_lon):
     taps = fine_taps()
     count = pert_fine.shape[0]
     members = count * lax.axis_size("mem")
@@ -56,7 +65,287 @@
     return (fine_total * factor, coarse_total * factor)
 
 
+def tap(d):
+    return np.where(np.abs(d) <= REACH, np.exp(-(d * d) / 32.0), 0.0)
+
+
+def constants(count, rows, block):
+    member = np.repeat(np.arange(count), rows)
+    row = np.tile(np.arange(rows), count)
+    own = (member[:, None] == member[None, :]) * tap(row[:, None] - row[None, :])
+    edge_member = np.tile(np.arange(count), REACH)
+    step = np.repeat(np.arange(REACH), count)
+    same = edge_member[:, None] == member[None, :]
+    to_next = same * tap(row[None, :] - (rows + step)[:, None])
+    to_before = same * tap(row[None, :] - (step - REACH)[:, None])
+    first = same * (row[None, :] == step[:, None])
+    last = same * (row[None, :] == (rows - REACH + step)[:, None])
+    half = block // 2
+    lon = tap(np.arange(2 * block)[:, None] - half - np.arange(block)[None, :])
+    spread = np.concatenate([to_next, to_before], 0)
+    pick = np.concatenate([first, last], 0)
+    return [jnp.asarray(a, BF16) for a in (own, spread, pick, lon)]
+
+
+def dot(a, b):
+    return jnp.dot(a, b, preferred_element_type=F32)
+
+
+def kernel(
+    bands, groups, block, factor,
+    v_fine, v_coarse, pert_fine, pert_coarse, gauss_lat, gauss_lon, own_m, spread_m, pick_m, lon_m,
+    out_fine, out_coarse,
+    vf, vc, pf, glat, glon, own, spread, pick, lon,
+    wide, weighted, halo_out, halo_in, edge, part, cpert, cv, cpart, crecv, zfine, zcoarse,
+    load, a_send, a_recv, v_send, v_recv, h_send, h_recv, c_send, c_recv, f_send, f_recv, z_send, z_recv,
+):
+    mem = lax.axis_index("mem")
+    lat = lax.axis_index("lat")
+    count, rows, width = pert_fine.shape
+    crows, cwidth = v_coarse.shape
+    mine = count // bands
+    edges = REACH * count
+
+    loads = [
+        pltpu.make_async_copy(src, dst, load.at[i])
+        for i, (src, dst) in enumerate(
+            [
+                (v_coarse, vc),
+                (pert_fine, pf),
+                (v_fine, vf),
+                (spread_m, spread),
+                (lon_m, lon),
+                (own_m, own),
+                (pick_m, pick),
+                (gauss_lon, glon),
+                (gauss_lat, glat),
+                (pert_coarse.at[pl.ds(lat * mine, mine)], cpert.at[lat]),
+            ]
+        )
+    ]
+    for copy in loads:
+        copy.start()
+
+    def peer_lat(o):
+        return lax.rem(lat + o, bands)
+
+    def peer_mem(o):
+        return lax.rem(mem + o, groups)
+
+    barrier = pltpu.get_barrier_semaphore()
+    for o in range(1, bands):
+        pl.semaphore_signal(barrier, inc=1, device_id=(mem, peer_lat(o)), device_id_type=MESH)
+    for o in range(1, groups):
+        pl.semaphore_signal(barrier, inc=1, device_id=(peer_mem(o), lat), device_id_type=MESH)
+    pl.semaphore_wait(barrier, bands - 1 + groups - 1)
+
+    def over_lat(o, src, dst, send, recv):
+        return pltpu.make_async_remote_copy(
+            src_ref=src, dst_ref=dst.at[lat], send_sem=send.at[o - 1], recv_sem=recv.at[lat],
+            device_id=(mem, peer_lat(o)), device_id_type=MESH,
+        )
+
+    def from_lat(o, dst, send, recv):
+        at = lax.rem(lat + bands - o, bands)
+        pltpu.make_async_remote_copy(
+            src_ref=dst.at[at], dst_ref=dst.at[at], send_sem=send.at[o - 1], recv_sem=recv.at[at],
+            device_id=(mem, peer_lat(o)), device_id_type=MESH,
+        ).wait_recv()
+
+    def over_mem(o, ref, send, recv):
+        return pltpu.make_async_remote_copy(
+            src_ref=ref.at[mem], dst_ref=ref.at[mem], send_sem=send.at[o - 1], recv_sem=recv.at[mem],
+            device_id=(peer_mem(o), lat), device_id_type=MESH,
+        )
+
+    def from_mem(o, ref, send, recv):
+        at = lax.rem(mem + groups - o, groups)
+        pltpu.make_async_remote_copy(
+            src_ref=ref.at[at], dst_ref=ref.at[at], send_sem=send.at[o - 1], recv_sem=recv.at[at],
+            device_id=(peer_mem(o), lat), device_id_type=MESH,
+        ).wait_recv()
+
+    sent = []
+
+    for o in range(1, bands):
+        copy = over_lat(o, pert_coarse.at[pl.ds(peer_lat(o) * mine, mine)], cpert, a_send, a_recv)
+        copy.start()
+        sent.append(copy)
+    loads[0].wait()
+    cv[lat] = vc[...].astype(BF16)
+    for o in range(1, bands):
+        copy = over_lat(o, cv.at[lat], cv, v_send, v_recv)
+        copy.start()
+        sent.append(copy)
+
+    for copy in loads[1:5]:
+        copy.wait()
+    weighted[...] = (pf[...].astype(F32) * vf[...][None]).astype(BF16).reshape(count * rows, width)
+    half = block // 2
+
+    def smooth(matrix, n):
+        along = dot(matrix, weighted[...]).astype(BF16)
+        wide[0:n, half : half + width] = along
+        wide[0:n, 0:half] = along[:, width - half :]
+        wide[0:n, half + width :] = along[:, :half]
+        for b in range(width // block):
+            yield b * block, dot(wide[0:n, b * block : (b + 2) * block], lon[...])
+
+    for at, value in smooth(spread[...], 2 * edges):
+        halo_out[:, :, at : at + block] = value.astype(BF16).reshape(2, edges, block)
+
+    def halo(side, target):
+        return pltpu.make_async_remote_copy(
+            src_ref=halo_out.at[side], dst_ref=halo_in.at[side],
+            send_sem=h_send.at[side], recv_sem=h_recv.at[side],
+            device_id=(mem, target), device_id_type=MESH,
+        )
+
+    @pl.when(lat < bands - 1)
+    def _():
+        halo(0, lat + 1).start()
+
+    @pl.when(lat > 0)
+    def _():
+        halo(1, lat - 1).start()
+
+    loads[5].wait()
+    for at, value in smooth(own[...], count * rows):
+        product = value.reshape(count, rows, block) * pf[:, :, at : at + block].astype(F32)
+        part[:, at : at + block] = jnp.sum(product, axis=0)
+    loads[6].wait()
+    edge[...] = dot(pick[...], pf[...].reshape(count * rows, width)).astype(BF16).reshape(2, edges, width)
+
+    for copy in loads[7:]:
+        copy.wait()
+    for o in range(1, bands):
+        from_lat(o, cpert, a_send, a_recv)
+    for o in range(1, bands):
+        from_lat(o, cv, v_send, v_recv)
+    total = jnp.zeros((bands * crows, cwidth), F32)
+    for j in range(mine):
+        pert = cpert[:, j].astype(F32).reshape(bands * crows, cwidth)
+        value = (pert * cv[...].astype(F32).reshape(bands * crows, cwidth)).astype(BF16)
+        value = lax.dot_general(value, glon[...], (((1,), (1,)), ((), ())), preferred_element_type=F32)
+        value = dot(glat[...], value.astype(BF16)).astype(BF16)
+        total = total + pert * value.astype(F32)
+    cpart[...] = total.astype(BF16).reshape(bands, crows, cwidth)
+    for o in range(1, bands):
+        copy = over_lat(o, cpart.at[peer_lat(o)], crecv, c_send, c_recv)
+        copy.start()
+        sent.append(copy)
+    crecv[lat] = cpart[lat]
+
+    @pl.when(lat > 0)
+    def _():
+        halo(0, lat - 1).wait_recv()
+        product = halo_in[0].astype(F32) * edge[0].astype(F32)
+        part[0:REACH] = part[0:REACH] + jnp.sum(product.reshape(REACH, count, width), axis=1)
+
+    @pl.when(lat < bands - 1)
+    def _():
+        halo(1, lat + 1).wait_recv()
+        product = halo_in[1].astype(F32) * edge[1].astype(F32)
+        part[rows - REACH :] = part[rows - REACH :] + jnp.sum(product.reshape(REACH, count, width), axis=1)
+
+    zfine[mem] = part[...].astype(BF16)
+    for o in range(1, groups):
+        copy = over_mem(o, zfine, f_send, f_recv)
+        copy.start()
+        sent.append(copy)
+
+    for o in range(1, bands):
+        from_lat(o, crecv, c_send, c_recv)
+    zcoarse[mem] = jnp.sum(crecv[...].astype(F32), axis=0).astype(BF16)
+    for o in range(1, groups):
+        copy = over_mem(o, zcoarse, z_send, z_recv)
+        copy.start()
+        sent.append(copy)
+
+    for o in range(1, groups):
+        from_mem(o, zfine, f_send, f_recv)
+    out_fine[...] = jnp.sum(zfine[...].astype(F32), axis=0) * factor
+    for o in range(1, groups):
+        from_mem(o, zcoarse, z_send, z_recv)
+    out_coarse[...] = jnp.sum(zcoarse[...].astype(F32), axis=0) * factor
+
+    for copy in sent:
+        copy.wait_send()
+
+    @pl.when(lat < bands - 1)
+    def _():
+        halo(0, lat + 1).wait_send()
+
+    @pl.when(lat > 0)
+    def _():
+        halo(1, lat - 1).wait_send()
+
+
+def fused(v_fine, v_coarse, pert_fine, pert_coarse, gauss_lat, gauss_lon):
+    bands, groups = lax.axis_size("lat"), lax.axis_size("mem")
+    count, rows, width = pert_fine.shape
+    crows, cwidth = v_coarse.shape
+    mine = count // bands
+    edges = REACH * count
+    block = 256
+    half = block // 2
+    mats = constants(count, rows, block)
+    dma = pltpu.SemaphoreType.DMA
+    vmem = pltpu.VMEM
+    return pl.pallas_call(
+        functools.partial(kernel, bands, groups, block, 1.0 / (count * groups - 1)),
+        out_shape=(
+            jax.ShapeDtypeStruct((rows, width), F32),
+            jax.ShapeDtypeStruct((crows, cwidth), F32),
+        ),
+        in_specs=[pl.BlockSpec(memory_space=pl.ANY)] * 10,
+        out_specs=[pl.BlockSpec(memory_space=pltpu.VMEM)] * 2,
+        scratch_shapes=[
+            vmem(v_fine.shape, F32),
+            vmem(v_coarse.shape, F32),
+            vmem(pert_fine.shape, BF16),
+            vmem(gauss_lat.shape, BF16),
+            vmem(gauss_lon.shape, BF16),
+            *[vmem(a.shape, BF16) for a in mats],
+            vmem((max(count * rows, 2 * edges), width + 2 * half), BF16),
+            vmem((count * rows, width), BF16),
+            vmem((2, edges, width), BF16),
+            vmem((2, edges, width), BF16),
+            vmem((2, edges, width), BF16),
+            vmem((rows, width), F32),
+            vmem((bands, mine, crows, cwidth), BF16),
+            vmem((bands, crows, cwidth), BF16),
+            vmem((bands, crows, cwidth), BF16),
+            vmem((bands, crows, cwidth), BF16),
+            vmem((groups, rows, width), BF16),
+            vmem((groups, crows, cwidth), BF16),
+            dma((10,)),
+            dma((bands,)), dma((bands,)),
+            dma((bands,)), dma((bands,)),
+            dma((2,)), dma((2,)),
+            dma((bands,)), dma((bands,)),
+            dma((groups,)), dma((groups,)),
+            dma((groups,)), dma((groups,)),
+        ],
+        compiler_params=pltpu.CompilerParams(
+            collective_id=0, has_side_effects=True, vmem_limit_bytes=60 * 1024 * 1024
+        ),
+        name="covariance",
+    )(v_fine, v_coarse, pert_fine, pert_coarse, gauss_lat, gauss_lon, *mats)
+
+
 def solution(mesh):
+    bands = mesh.shape["lat"]
+    groups = mesh.shape["mem"]
+
+    def local(v_fine, v_coarse, pert_fine, pert_coarse, gauss_lat, gauss_lon):
+        count, rows, width = pert_fine.shape
+        crows, cwidth = v_coarse.shape
+        even = count % bands == 0 and count % 16 == 0 and crows % 16 == 0 and cwidth % 128 == 0
+        if bands > 1 and groups > 1 and even and rows % 16 == 0 and width % 256 == 0:
+            return fused(v_fine, v_coarse, pert_fine, pert_coarse, gauss_lat, gauss_lon)
+        return general(v_fine, v_coarse, pert_fine, pert_coarse, gauss_lat, gauss_lon)
+
     placed = (
         P("lat", None),
         P("lat", None),

time: 95.1 us -> 24.5 us (0.26)
  waiting for transfers between devices: 42.9 us -> 0 us
  Pallas kernels: 0 us -> 21.6 us
  blocking collectives: 17.8 us -> 0 us
  between operations: 15.7 us -> 0.65 us
  other arithmetic: 8.65 us -> 0 us
  starting transfers between devices: 3.75 us -> 0 us
  matrix products: 3.03 us -> 0 us
    psum x1 -> x0, waiting for transfers between devices: 38.7 us -> none  [local(): fine_total, coarse_total = lax.psum((fine_part, coarse_part), 'mem')]
    pallas_call x0 -> x1, Pallas kernels: none -> 21.6 us  [fused(): pl.pallas_call(functools.partial(kernel, bands, groups, block, 1.0 / (cou...]
    psum x1 -> x0, blocking collectives: 17.8 us -> none  [local(): fine_total, coarse_total = lax.psum((fine_part, coarse_part), 'mem')]
    ppermute x2 -> x0, waiting for transfers between devices: 4.13 us -> none  [the longest x1 4.13 us: extended(): after = lax.ppermute(leading, axis, down)]
    ppermute x2 -> x0, starting transfers between devices: 3.66 us -> none  [the longest x1 2.37 us: extended(): before = lax.ppermute(last, axis, up)]
    reduce_sum x1 -> x0, other arithmetic: 3.19 us -> none  [local(): fine_part = jnp.sum(pert_fine.astype(jnp.float32) * across, axis=0)]
    dot_general x2 -> x0, matrix products: 3.03 us -> none  [the longest x1 2.08 us: local(): jnp.einsum('rj,mjc->mrc', band, lax.all_gather(ctrans, 'lat', axis=1, til...]
    slice x11 -> x0, local copies, waits for them, and re-layouts: 2.49 us -> none  [the longest x10 2.41 us: local(): across = across + taps[offset] * jnp.roll(along, offset - 5, axis=2)]
  transfers between devices with their start and end apart: 4 -> 0, of which waited for: 2 -> 0; matrix products, arithmetic and copies ran while one was open for 3% -> 0% of each run, Pallas kernels for 0% -> 0%
where the time goes in v1:
time: 24.5 us; the launch traced here: 24.4 us
  Pallas kernels  21.6 us (88%)
  local copies, waits for them, and re-layouts  2.1 us (9%)
  between operations  0.65 us (3%)
    pallas_call x1, Pallas kernels, fused(): pl.pallas_call(functools.partial(kernel, bands, groups, block, 1.0 / (cou...  21.6 us
    unnamed x4, local copies, waits for them, and re-layouts  2.1 us

profile of v1, /device:TPU:0, one launch (start us, length us, event | category | flops | bytes accessed | tf_op | source)
XLA Modules:
  0.0 24.4 jit_solution(12442936276079473259)
XLA Ops:
  0.6 21.6 %covariance.1 = (f32[16,1024]{1,0:T(8,128)}, f32[32,256]{1,0:T(8,128)}) custom-call(f32[16,1024]{1,0:T(8,128)} %v_fine.1, f32[32,256]{1,0:T(8,128)} %v_coarse.1, bf16[16,16,1024]{2,1,0:T(8,128)(2,1)} %pert_fine.1, bf16[16,32,256]{2,1,0:T(8,128)(2,1)} %pert_coarse.1, bf16[256,256]{1,0:T(8,128)(2,1)} %gauss_lat.1, bf16[256,256]{1,0:T(8,128)(2,1)} %gauss_lon.1, ...), custom_call_target="tpu_custom_call" | custom-call | tf_op jit(solution)/shard_map/covariance/pallas_call | solution.py:295
  22.3 0.0 copy-start
  22.3 1.5 %copy.14 = f32[16,1024]{1,0:T(8,128)} copy(f32[16,1024]{1,0:T(8,128)} %get-tuple-element.4) | data formatting | bytes 131072
  23.8 0.0 copy-done
  23.8 0.6 %copy.15 = f32[32,256]{1,0:T(8,128)} copy(f32[32,256]{1,0:T(8,128)S(1)} %copy-done) | data formatting | bytes 65536
Async XLA Ops:
  22.3 1.5 %copy-start = (f32[32,256]{1,0:T(8,128)S(1)}, f32[32,256]{1,0:T(8,128)}, u32[]{:S(2)}) copy-start(f32[32,256]{1,0:T(8,128)} %get-tuple-element.5) | copy-start | bytes 98308

commit v2 on v1

--- a/solution.py
+++ b/solution.py
@@ -96,8 +96,8 @@
     v_fine, v_coarse, pert_fine, pert_coarse, gauss_lat, gauss_lon, own_m, spread_m, pick_m, lon_m,
     out_fine, out_coarse,
     vf, vc, pf, glat, glon, own, spread, pick, lon,
-    wide, weighted, halo_out, halo_in, edge, part, cpert, cv, cpart, crecv, zfine, zcoarse,
-    load, a_send, a_recv, v_send, v_recv, h_send, h_recv, c_send, c_recv, f_send, f_recv, z_send, z_recv,
+    wide, weighted, halo_out, halo_in, edge, part, pc, cout, cin, sout, sin, zfine, zcoarse,
+    load, a_send, a_recv, h_send, h_recv, c_send, c_recv, f_send, f_recv, z_send, z_recv,
 ):
     mem = lax.axis_index("mem")
     lat = lax.axis_index("lat")
@@ -111,6 +111,7 @@
         for i, (src, dst) in enumerate(
             [
                 (v_coarse, vc),
+                (pert_coarse, pc),
                 (pert_fine, pf),
                 (v_fine, vf),
                 (spread_m, spread),
@@ -119,7 +120,6 @@
                 (pick_m, pick),
                 (gauss_lon, glon),
                 (gauss_lat, glat),
-                (pert_coarse.at[pl.ds(lat * mine, mine)], cpert.at[lat]),
             ]
         )
     ]
@@ -167,18 +167,17 @@
 
     sent = []
 
-    for o in range(1, bands):
-        copy = over_lat(o, pert_coarse.at[pl.ds(peer_lat(o) * mine, mine)], cpert, a_send, a_recv)
+    for copy in loads[:2]:
+        copy.wait()
+    cweighted = (pc[...].astype(F32) * vc[...][None]).astype(BF16)
+    cout[...] = cweighted.reshape(bands, mine, crows, cwidth)
+    for o in range(1, bands):
+        copy = over_lat(o, cout.at[peer_lat(o)], cin, a_send, a_recv)
         copy.start()
         sent.append(copy)
-    loads[0].wait()
-    cv[lat] = vc[...].astype(BF16)
-    for o in range(1, bands):
-        copy = over_lat(o, cv.at[lat], cv, v_send, v_recv)
-        copy.start()
-        sent.append(copy)
-
-    for copy in loads[1:5]:
+    cin[lat] = cout[lat]
+
+    for copy in loads[2:6]:
         copy.wait()
     weighted[...] = (pf[...].astype(F32) * vf[...][None]).astype(BF16).reshape(count * rows, width)
     half = block // 2
@@ -209,32 +208,27 @@
     def _():
         halo(1, lat - 1).start()
 
-    loads[5].wait()
+    loads[6].wait()
     for at, value in smooth(own[...], count * rows):
         product = value.reshape(count, rows, block) * pf[:, :, at : at + block].astype(F32)
         part[:, at : at + block] = jnp.sum(product, axis=0)
-    loads[6].wait()
+    loads[7].wait()
     edge[...] = dot(pick[...], pf[...].reshape(count * rows, width)).astype(BF16).reshape(2, edges, width)
 
-    for copy in loads[7:]:
+    for copy in loads[8:]:
         copy.wait()
     for o in range(1, bands):
-        from_lat(o, cpert, a_send, a_recv)
-    for o in range(1, bands):
-        from_lat(o, cv, v_send, v_recv)
-    total = jnp.zeros((bands * crows, cwidth), F32)
+        from_lat(o, cin, a_send, a_recv)
     for j in range(mine):
-        pert = cpert[:, j].astype(F32).reshape(bands * crows, cwidth)
-        value = (pert * cv[...].astype(F32).reshape(bands * crows, cwidth)).astype(BF16)
+        value = cin[:, j].reshape(bands * crows, cwidth)
         value = lax.dot_general(value, glon[...], (((1,), (1,)), ((), ())), preferred_element_type=F32)
         value = dot(glat[...], value.astype(BF16)).astype(BF16)
-        total = total + pert * value.astype(F32)
-    cpart[...] = total.astype(BF16).reshape(bands, crows, cwidth)
-    for o in range(1, bands):
-        copy = over_lat(o, cpart.at[peer_lat(o)], crecv, c_send, c_recv)
+        sout[:, j] = value.reshape(bands, crows, cwidth)
+    for o in range(1, bands):
+        copy = over_lat(o, sout.at[peer_lat(o)], sin, c_send, c_recv)
         copy.start()
         sent.append(copy)
-    crecv[lat] = cpart[lat]
+    sin[lat] = sout[lat]
 
     @pl.when(lat > 0)
     def _():
@@ -255,8 +249,9 @@
         sent.append(copy)
 
     for o in range(1, bands):
-        from_lat(o, crecv, c_send, c_recv)
-    zcoarse[mem] = jnp.sum(crecv[...].astype(F32), axis=0).astype(BF16)
+        from_lat(o, sin, c_send, c_recv)
+    smoothed = sin[...].reshape(count, crows, cwidth).astype(F32)
+    zcoarse[mem] = jnp.sum(pc[...].astype(F32) * smoothed, axis=0).astype(BF16)
     for o in range(1, groups):
         copy = over_mem(o, zcoarse, z_send, z_recv)
         copy.start()
@@ -313,14 +308,11 @@
             vmem((2, edges, width), BF16),
             vmem((2, edges, width), BF16),
             vmem((rows, width), F32),
-            vmem((bands, mine, crows, cwidth), BF16),
-            vmem((bands, crows, cwidth), BF16),
-            vmem((bands, crows, cwidth), BF16),
-            vmem((bands, crows, cwidth), BF16),
+            vmem(pert_coarse.shape, BF16),
+            *[vmem((bands, mine, crows, cwidth), BF16)] * 4,
             vmem((groups, rows, width), BF16),
             vmem((groups, crows, cwidth), BF16),
             dma((10,)),
-            dma((bands,)), dma((bands,)),
             dma((bands,)), dma((bands,)),
             dma((2,)), dma((2,)),
             dma((bands,)), dma((bands,)),

time: 24.5 us -> 23.8 us (0.971)
  Pallas kernels: 21.6 us -> 20.9 us
    pallas_call x1, Pallas kernels: 21.6 us -> 20.9 us  [fused(): pl.pallas_call(functools.partial(kernel, bands, groups, block, 1.0 / (cou...]
where the time goes in v2:
time: 23.8 us; the launch traced here: 23.7 us
  Pallas kernels  20.9 us (88%)
  local copies, waits for them, and re-layouts  2.1 us (9%)
  between operations  0.65 us (3%)
    pallas_call x1, Pallas kernels, fused(): pl.pallas_call(functools.partial(kernel, bands, groups, block, 1.0 / (cou...  20.9 us
    unnamed x4, local copies, waits for them, and re-layouts  2.1 us

profile of v2, /device:TPU:0, one launch (start us, length us, event | category | flops | bytes accessed | tf_op | source)
XLA Modules:
  0.0 23.7 jit_solution(12253642770513517326)
XLA Ops:
  0.6 20.9 %covariance.1 = (f32[16,1024]{1,0:T(8,128)}, f32[32,256]{1,0:T(8,128)}) custom-call(f32[16,1024]{1,0:T(8,128)} %v_fine.1, f32[32,256]{1,0:T(8,128)} %v_coarse.1, bf16[16,16,1024]{2,1,0:T(8,128)(2,1)} %pert_fine.1, bf16[16,32,256]{2,1,0:T(8,128)(2,1)} %pert_coarse.1, bf16[256,256]{1,0:T(8,128)(2,1)} %gauss_lat.1, bf16[256,256]{1,0:T(8,128)(2,1)} %gauss_lon.1, ...), custom_call_target="tpu_custom_call" | custom-call | tf_op jit(solution)/shard_map/covariance/pallas_call | solution.py:290
  21.6 0.0 copy-start
  21.6 1.5 %copy.14 = f32[16,1024]{1,0:T(8,128)} copy(f32[16,1024]{1,0:T(8,128)} %get-tuple-element.4) | data formatting | bytes 131072
  23.1 0.0 copy-done
  23.1 0.6 %copy.15 = f32[32,256]{1,0:T(8,128)} copy(f32[32,256]{1,0:T(8,128)S(1)} %copy-done) | data formatting | bytes 65536
Async XLA Ops:
  21.6 1.5 %copy-start = (f32[32,256]{1,0:T(8,128)S(1)}, f32[32,256]{1,0:T(8,128)}, u32[]{:S(2)}) copy-start(f32[32,256]{1,0:T(8,128)} %get-tuple-element.5) | copy-start | bytes 98308

commit v3 on v2

--- a/solution.py
+++ b/solution.py
@@ -137,20 +137,32 @@
         pl.semaphore_signal(barrier, inc=1, device_id=(mem, peer_lat(o)), device_id_type=MESH)
     for o in range(1, groups):
         pl.semaphore_signal(barrier, inc=1, device_id=(peer_mem(o), lat), device_id_type=MESH)
+
+    for copy in loads[:2]:
+        copy.wait()
+    for j in range(mine):
+        for b in range(bands):
+            cout[j, b] = (pc[b * mine + j].astype(F32) * vc[...]).astype(BF16)
+    for j in range(mine):
+        cin[j, lat] = cout[j, lat]
+
     pl.semaphore_wait(barrier, bands - 1 + groups - 1)
 
-    def over_lat(o, src, dst, send, recv):
+    def over_lat(j, o, src, dst, send, recv):
         return pltpu.make_async_remote_copy(
-            src_ref=src, dst_ref=dst.at[lat], send_sem=send.at[o - 1], recv_sem=recv.at[lat],
+            src_ref=src.at[j, peer_lat(o)], dst_ref=dst.at[j, lat],
+            send_sem=send.at[j, o - 1], recv_sem=recv.at[j, lat],
             device_id=(mem, peer_lat(o)), device_id_type=MESH,
         )
 
-    def from_lat(o, dst, send, recv):
+    def from_lat(j, o, dst, send, recv):
         at = lax.rem(lat + bands - o, bands)
         pltpu.make_async_remote_copy(
-            src_ref=dst.at[at], dst_ref=dst.at[at], send_sem=send.at[o - 1], recv_sem=recv.at[at],
+            src_ref=dst.at[j, at], dst_ref=dst.at[j, at],
+            send_sem=send.at[j, o - 1], recv_sem=recv.at[j, at],
             device_id=(mem, peer_lat(o)), device_id_type=MESH,
         ).wait_recv()
+        return at
 
     def over_mem(o, ref, send, recv):
         return pltpu.make_async_remote_copy(
@@ -167,15 +179,11 @@
 
     sent = []
 
-    for copy in loads[:2]:
-        copy.wait()
-    cweighted = (pc[...].astype(F32) * vc[...][None]).astype(BF16)
-    cout[...] = cweighted.reshape(bands, mine, crows, cwidth)
-    for o in range(1, bands):
-        copy = over_lat(o, cout.at[peer_lat(o)], cin, a_send, a_recv)
-        copy.start()
-        sent.append(copy)
-    cin[lat] = cout[lat]
+    for j in range(mine):
+        for o in range(1, bands):
+            copy = over_lat(j, o, cout, cin, a_send, a_recv)
+            copy.start()
+            sent.append(copy)
 
     for copy in loads[2:6]:
         copy.wait()
@@ -217,18 +225,17 @@
 
     for copy in loads[8:]:
         copy.wait()
-    for o in range(1, bands):
-        from_lat(o, cin, a_send, a_recv)
-    for j in range(mine):
-        value = cin[:, j].reshape(bands * crows, cwidth)
+    for j in range(mine):
+        for o in range(1, bands):
+            from_lat(j, o, cin, a_send, a_recv)
+        value = cin[j].reshape(bands * crows, cwidth)
         value = lax.dot_general(value, glon[...], (((1,), (1,)), ((), ())), preferred_element_type=F32)
         value = dot(glat[...], value.astype(BF16)).astype(BF16)
-        sout[:, j] = value.reshape(bands, crows, cwidth)
-    for o in range(1, bands):
-        copy = over_lat(o, sout.at[peer_lat(o)], sin, c_send, c_recv)
-        copy.start()
-        sent.append(copy)
-    sin[lat] = sout[lat]
+        sout[j] = value.reshape(bands, crows, cwidth)
+        for o in range(1, bands):
+            copy = over_lat(j, o, sout, sin, c_send, c_recv)
+            copy.start()
+            sent.append(copy)
 
     @pl.when(lat > 0)
     def _():
@@ -248,10 +255,14 @@
         copy.start()
         sent.append(copy)
 
-    for o in range(1, bands):
-        from_lat(o, sin, c_send, c_recv)
-    smoothed = sin[...].reshape(count, crows, cwidth).astype(F32)
-    zcoarse[mem] = jnp.sum(pc[...].astype(F32) * smoothed, axis=0).astype(BF16)
+    total = jnp.zeros((crows, cwidth), F32)
+    for j in range(mine):
+        total = total + pc[lat * mine + j].astype(F32) * sout[j, lat].astype(F32)
+    for j in range(mine):
+        for o in range(1, bands):
+            at = from_lat(j, o, sin, c_send, c_recv)
+            total = total + pc[at * mine + j].astype(F32) * sin[j, at].astype(F32)
+    zcoarse[mem] = total.astype(BF16)
     for o in range(1, groups):
         copy = over_mem(o, zcoarse, z_send, z_recv)
         copy.start()
@@ -309,13 +320,13 @@
             vmem((2, edges, width), BF16),
             vmem((rows, width), F32),
             vmem(pert_coarse.shape, BF16),
-            *[vmem((bands, mine, crows, cwidth), BF16)] * 4,
+            *[vmem((mine, bands, crows, cwidth), BF16)] * 4,
             vmem((groups, rows, width), BF16),
             vmem((groups, crows, cwidth), BF16),
             dma((10,)),
-            dma((bands,)), dma((bands,)),
+            dma((mine, bands)), dma((mine, bands)),
             dma((2,)), dma((2,)),
-            dma((bands,)), dma((bands,)),
+            dma((mine, bands)), dma((mine, bands)),
             dma((groups,)), dma((groups,)),
             dma((groups,)), dma((groups,)),
         ],

time: 23.8 us -> 24.2 us (1.017)
  Pallas kernels: 20.9 us -> 21.3 us
    pallas_call x1, Pallas kernels: 20.9 us -> 21.3 us  [fused(): pl.pallas_call(functools.partial(kernel, bands, groups, block, 1.0 / (cou...]
where the time goes in v3:
time: 24.2 us; the launch traced here: 24.1 us
  Pallas kernels  21.3 us (88%)
  local copies, waits for them, and re-layouts  2.1 us (9%)
  between operations  0.65 us (3%)
    pallas_call x1, Pallas kernels, fused(): pl.pallas_call(functools.partial(kernel, bands, groups, block, 1.0 / (cou...  21.3 us
    unnamed x4, local copies, waits for them, and re-layouts  2.1 us

profile of v3, /device:TPU:0, one launch (start us, length us, event | category | flops | bytes accessed | tf_op | source)
XLA Modules:
  0.0 24.1 jit_solution(5492972084238472755)
XLA Ops:
  0.6 21.3 %covariance.1 = (f32[16,1024]{1,0:T(8,128)}, f32[32,256]{1,0:T(8,128)}) custom-call(f32[16,1024]{1,0:T(8,128)} %v_fine.1, f32[32,256]{1,0:T(8,128)} %v_coarse.1, bf16[16,16,1024]{2,1,0:T(8,128)(2,1)} %pert_fine.1, bf16[16,32,256]{2,1,0:T(8,128)(2,1)} %pert_coarse.1, bf16[256,256]{1,0:T(8,128)(2,1)} %gauss_lat.1, bf16[256,256]{1,0:T(8,128)(2,1)} %gauss_lon.1, ...), custom_call_target="tpu_custom_call" | custom-call | tf_op jit(solution)/shard_map/covariance/pallas_call | solution.py:301
  22.0 0.0 copy-start
  22.0 1.5 %copy.14 = f32[16,1024]{1,0:T(8,128)} copy(f32[16,1024]{1,0:T(8,128)} %get-tuple-element.4) | data formatting | bytes 131072
  23.4 0.0 copy-done
  23.4 0.6 %copy.15 = f32[32,256]{1,0:T(8,128)} copy(f32[32,256]{1,0:T(8,128)S(1)} %copy-done) | data formatting | bytes 65536
Async XLA Ops:
  22.0 1.5 %copy-start = (f32[32,256]{1,0:T(8,128)S(1)}, f32[32,256]{1,0:T(8,128)}, u32[]{:S(2)}) copy-start(f32[32,256]{1,0:T(8,128)} %get-tuple-element.5) | copy-start | bytes 98308
